TPU v7x, 256 devices: a whole 4x4x8 slice. The times are simulated.
256 devices in a mesh: grp: 16 (over z, y_hi), ep: 16 (over y_lo, x, core).
Axes of the slice: x: 4, y: 4 (y_hi: 2, y_lo: 2; y = y_hi * 2 + y_lo), z: 8, core: 2. Of those that a mesh axis runs over, the one named last changes fastest.
Arguments:
- tokens: bfloat16 [49152, 4096], P(('grp', 'ep')), may hold values from -6 to 6
- expert_ids: int32 [49152, 8], P(('grp', 'ep')), may hold values from 0 to 127, all different within a row; in each aligned block of 192 rows (0 to 191, 192 to 383, ...) at most 24 rows name the same one
- gate_probs: float32 [49152, 8], P(('grp', 'ep')), may hold values from 0.02 to 0.25
- placement: int32 [16, 4], P('grp'), may hold values from 0 to 1
- gate_weight: bfloat16 [16, 4096, 3072], P('grp', None, 'ep'), may hold values from -0.09375 to 0.09375
- up_weight: bfloat16 [16, 4096, 3072], P('grp', None, 'ep'), may hold values from -0.09375 to 0.09375
- down_weight: bfloat16 [16, 3072, 4096], P('grp', 'ep'), may hold values from -0.21875 to 0.21875
- out_grad: bfloat16 [49152, 4096], P(('grp', 'ep')), may hold values from -6 to 6
- moment_first: float32 [2, 3072, 4096], P(None, 'ep', 'grp'), may hold values from -2 to 2
- moment_second: float32 [2, 3072, 4096], P(None, 'ep', 'grp'), may hold values from 0.01 to 1
Outputs:
- token_grad: bfloat16 [49152, 4096], P(('grp', 'ep'))
- step_dir: bfloat16 [16, 3072, 4096], P('grp', 'ep')
- new_first: float32 [2, 3072, 4096], P(None, 'ep', 'grp')
- new_second: float32 [2, 3072, 4096], P(None, 'ep', 'grp')
Inputs may be any that keep to these rules, and one draw needn't show every extreme that they name: `expert_ids`: each row names 8 different experts. In the rows of one device no expert is named more than 24 times, a bound that some block reaches. Group g holds expert placement[g, s] * 4 + s in its slot s.
All inputs are finite; a program needn't handle non-finite values.
Results may differ from a plain program's by a relative error of at most 0.015.
Values may be sent and summed in bfloat16 or wider, within the bound.
A program may use at most 128 MiB of HBM per device.

v0:
```python
import math
import jax
import jax.numpy as jnp
from jax import lax
from jax.sharding import PartitionSpec as P

QUARTERS = 4
CANDS = 2
CAP = 24
beta_one = 0.9
beta_two = 0.999
adam_eps = 1e-08
first_fix = 1.0 - math.exp(1000.0 * math.log(0.9))
second_fix = 1.0 - math.exp(1000.0 * math.log(0.999))


def moments(gradient, first_moment, second):
    new_first = beta_one * first_moment + (1.0 - beta_one) * gradient
    new_second = beta_two * second + (1.0 - beta_two) * gradient * gradient
    return (new_first, new_second)


def direction(new_first, new_second):
    return new_first / first_fix / (jnp.sqrt(new_second / second_fix) + adam_eps)


def body(
    tokens,
    expert_ids,
    gate_probs,
    placement,
    gate_weight,
    up_weight,
    down_weight,
    out_grad,
    moment_first,
    moment_second,
):
    num_ep = lax.axis_size("ep")
    slot_count = num_ep // QUARTERS
    tok_count = tokens.shape[0]
    width = tokens.shape[1]
    held_ids = placement[0] * slot_count + jnp.arange(slot_count, dtype=jnp.int32)
    matches = expert_ids[:, :, None] == held_ids[None, None, :]
    hit_rows = jnp.any(matches, axis=1)
    coeffs = jnp.sum(jnp.where(matches, gate_probs[:, :, None], jnp.float32(0.0)), axis=1)
    ranking = jnp.cumsum(hit_rows.astype(jnp.int32), axis=0) - 1
    select_mask = hit_rows.T[:, None, :] & (
        ranking.T[:, None, :] == jnp.arange(CAP, dtype=jnp.int32)[None, :, None]
    )
    select_flat = select_mask.reshape(slot_count * CAP, tok_count).astype(jnp.bfloat16)
    send_tokens = jnp.dot(select_flat, tokens, preferred_element_type=jnp.float32).astype(
        jnp.bfloat16
    )
    send_grads = jnp.dot(select_flat, out_grad, preferred_element_type=jnp.float32).astype(
        jnp.bfloat16
    )
    send_coeffs = jnp.sum(select_mask.astype(jnp.float32) * coeffs.T[:, None, :], axis=2)

    def spread(source):
        shaped = source.reshape(slot_count, 1, CAP, width)
        return jnp.broadcast_to(shaped, (slot_count, QUARTERS, CAP, width)).reshape(
            num_ep, CAP, width
        )

    coeff_spread = jnp.broadcast_to(send_coeffs[:, None, :], (slot_count, QUARTERS, CAP)).reshape(
        num_ep, CAP
    )
    w_gate = gate_weight[0]
    w_up = up_weight[0]
    w_down = down_weight[0]
    recv_tokens, recv_grads, recv_coeffs = (
        lax.all_to_all(spread(send_tokens), "ep", split_axis=0, concat_axis=0, tiled=True),
        lax.all_to_all(spread(send_grads), "ep", split_axis=0, concat_axis=0, tiled=True),
        lax.all_to_all(
            coeff_spread.astype(jnp.bfloat16), "ep", split_axis=0, concat_axis=0, tiled=True
        ).astype(coeff_spread.dtype),
    )
    in_rows = recv_tokens.reshape(num_ep * CAP, width)
    pre_gate = jnp.dot(in_rows, w_gate, preferred_element_type=jnp.float32)
    pre_up = jnp.dot(in_rows, w_up, preferred_element_type=jnp.float32)
    sigmoid_gate = jax.nn.sigmoid(pre_gate)
    activated = pre_gate * sigmoid_gate
    hidden = (activated * pre_up).astype(jnp.bfloat16)
    pre_gate, pre_up, sigmoid_gate, activated, hidden = (
        pre_gate,
        pre_up,
        sigmoid_gate,
        activated,
        hidden,
    )
    scaled = (
        recv_coeffs.reshape(num_ep * CAP)[:, None]
        * recv_grads.reshape(num_ep * CAP, width).astype(jnp.float32)
    ).astype(jnp.bfloat16)
    d_hidden = jnp.einsum("rd,hd->rh", scaled, w_down, preferred_element_type=jnp.float32)
    weight_grad = jnp.einsum("rh,rd->hd", hidden, scaled, preferred_element_type=jnp.float32)
    d_gate = (d_hidden * pre_up * sigmoid_gate * (1.0 + pre_gate * (1.0 - sigmoid_gate))).astype(
        jnp.bfloat16
    )
    d_up = (d_hidden * activated).astype(jnp.bfloat16)
    partial_value = jnp.einsum("rh,dh->rd", d_gate, w_gate, preferred_element_type=jnp.float32)
    partial_value = (
        partial_value + jnp.einsum("rh,dh->rd", d_up, w_up, preferred_element_type=jnp.float32)
    ).astype(jnp.bfloat16)
    returned = lax.all_to_all(
        partial_value.reshape(num_ep, CAP, width), "ep", split_axis=0, concat_axis=0, tiled=True
    )
    combine = jnp.broadcast_to(
        select_mask.reshape(slot_count, 1, CAP, tok_count), (slot_count, QUARTERS, CAP, tok_count)
    )
    combine = combine.reshape(num_ep * CAP, tok_count).astype(jnp.bfloat16)
    token_grad = jnp.einsum(
        "kt,kd->td",
        combine,
        returned.reshape(num_ep * CAP, width),
        preferred_element_type=jnp.float32,
    ).astype(jnp.bfloat16)
    ep_index = lax.axis_index("ep")
    my_cand = lax.dynamic_index_in_dim(placement[0], ep_index // QUARTERS, 0, keepdims=False)
    cand_mask = (jnp.arange(CANDS, dtype=jnp.int32) == my_cand).astype(jnp.float32)
    cand_grads = cand_mask[:, None, None] * weight_grad[None]
    totals = lax.psum(cand_grads.astype(jnp.bfloat16), "grp").astype(jnp.float32)
    full_first, full_second = (
        lax.all_gather(moment_first.astype(jnp.bfloat16), "grp", axis=2, tiled=True).astype(
            moment_first.dtype
        ),
        lax.all_gather(moment_second.astype(jnp.bfloat16), "grp", axis=2, tiled=True).astype(
            moment_second.dtype
        ),
    )
    share_cols = moment_first.shape[2]
    share_start = lax.axis_index("grp") * share_cols
    new_first, new_second = moments(
        lax.dynamic_slice_in_dim(totals, share_start, share_cols, 2), moment_first, moment_second
    )
    own_grad = lax.dynamic_index_in_dim(totals, my_cand, 0, keepdims=True)
    own_first = lax.dynamic_index_in_dim(full_first, my_cand, 0, keepdims=True)
    own_second = lax.dynamic_index_in_dim(full_second, my_cand, 0, keepdims=True)
    copy_first, copy_second = moments(own_grad, own_first, own_second)
    step_dir = direction(copy_first, copy_second).astype(jnp.bfloat16)
    return (token_grad, step_dir, new_first, new_second)


def solution(mesh):
    return jax.shard_map(
        body,
        mesh=mesh,
        in_specs=(
            P(("grp", "ep"), None),
            P(("grp", "ep"), None),
            P(("grp", "ep"), None),
            P("grp", None),
            P("grp", None, "ep"),
            P("grp", None, "ep"),
            P("grp", "ep", None),
            P(("grp", "ep"), None),
            P(None, "ep", "grp"),
            P(None, "ep", "grp"),
        ),
        out_specs=(
            P(("grp", "ep"), None),
            P("grp", "ep", None),
            P(None, "ep", "grp"),
            P(None, "ep", "grp"),
        ),
        check_vma=False,
    )
```

profile of v0, /device:TPU:2, one launch (start us, length us, event | category | flops | bytes accessed | tf_op | source)
XLA Modules:
  0.0 527.4 jit_solution(9174069582011565920)
XLA Ops:
  8.0 0.8 compare_reduce_fusion
  8.7 0.8 fusion.24
  9.6 1.2 reduce-window.6
  11.9 5.9 %all-to-all-start = ((bf16[16,1,24]{2,1,0:T(2,128)(2,1)}), bf16[16,1,24]{2,1,0:T(2,128)(2,1)S(1)}, u32[]{:S(2)}, u32[]{:S(2)}) async-start(bf16[16,1,24]{2,1,0:T(2,128)(2,1)} %copy.29), calls=%async_computation | async-start | bytes 16384 | tf_op jit(solution)/shard_map/all_to_all | solution.py:75
  18.0 1.8 convolution_convert_fusion.1
  19.8 2.6 all-to-all-done
  22.4 2.1 broadcast_in_dim.53
  24.5 5.7 %all-to-all-start.2 = ((bf16[16,24,4096]{2,1,0:T(8,128)(2,1)}), bf16[16,24,4096]{2,1,0:T(8,128)(2,1)}, u32[]{:S(2)}, u32[]{:S(2)}) async-start(bf16[16,24,4096]{2,1,0:T(8,128)(2,1)} %bitcast.62), calls=%async_computation.2 | async-start | bytes 6291456 | tf_op jit(solution)/shard_map/all_to_all | solution.py:73
  30.2 1.8 convolution_convert_fusion.2
  31.9 41.2 %all-to-all-done.2 = bf16[16,24,4096]{2,1,0:T(8,128)(2,1)} async-done(((bf16[16,24,4096]{2,1,0:T(8,128)(2,1)}), bf16[16,24,4096]{2,1,0:T(8,128)(2,1)}, u32[]{:S(2)}, u32[]{:S(2)}) %all-to-all-start.2) | async-done | bytes 3145760 | tf_op jit(solution)/shard_map/all_to_all | solution.py:73
  73.1 2.1 broadcast_in_dim.29
  75.2 4.5 all-to-all-start.1
  81.1 3.1 fusion.9
  84.2 3.8 fusion.12
  88.0 34.3 %all-to-all-done.1 = bf16[16,24,4096]{2,1,0:T(8,128)(2,1)} async-done(((bf16[16,24,4096]{2,1,0:T(8,128)(2,1)}), bf16[16,24,4096]{2,1,0:T(8,128)(2,1)}, u32[]{:S(2)}, u32[]{:S(2)}) %all-to-all-start.1) | async-done | bytes 3145760 | tf_op jit(solution)/shard_map/all_to_all | solution.py:74
  122.3 2.9 fusion
  125.3 1.0 fusion.18
  126.3 2.3 multiply_convert_fusion
  128.6 181.3 %all-reduce.3.cloned.1.call-done = bf16[2,192,4096]{2,1,0:T(8,128)(2,1)} async-done(((bf16[2,192,4096]{2,1,0:T(8,128)(2,1)}), bf16[2,192,4096]{2,1,0:T(8,128)(2,1)}) %all-reduce.3.cloned.1.call-update) | async-done | bytes 3145744 | tf_op jit(solution)/shard_map/psum | solution.py:123
  309.9 2.7 convert_element_type.124
  312.7 2.7 copy-done.1
  315.3 1.1 fusion.16
  317.2 3.0 multiply_convert_fusion.1
  320.2 1.2 fusion.14
  321.5 1.1 fusion.7
  322.5 2.7 add_convert_fusion
  325.3 4.6 all-to-all-start.3
  331.8 40.9 %all-to-all-done.3 = bf16[16,24,4096]{2,1,0:T(8,128)(2,1)} async-done(((bf16[16,24,4096]{2,1,0:T(8,128)(2,1)}), bf16[16,24,4096]{2,1,0:T(8,128)(2,1)}, u32[]{:S(2)}, u32[]{:S(2)}) %all-to-all-start.3) | async-done | bytes 3145760 | tf_op jit(solution)/shard_map/all_to_all | solution.py:106
  372.8 4.1 convolution_convert_fusion
  376.8 43.8 %all-gather.3.cloned.1.call-done = bf16[2,192,4096]{2,1,0:T(8,128)(2,1)} async-done(((bf16[2,192,256]{2,1,0:T(8,128)(2,1)}), bf16[2,192,4096]{2,1,0:T(8,128)(2,1)}) %all-gather.3.cloned.1.call-update) | async-done | bytes 3145744 | tf_op jit(solution)/shard_map/all_gather | solution.py:125
  420.7 94.2 %all-gather.5.cloned.1.call-done = bf16[2,192,4096]{2,1,0:T(8,128)(2,1)} async-done(((bf16[2,192,256]{2,1,0:T(8,128)(2,1)}), bf16[2,192,4096]{2,1,0:T(8,128)(2,1)}) %all-gather.5.cloned.1.call-update) | async-done | bytes 3145744 | tf_op jit(solution)/shard_map/all_gather | solution.py:128
  514.8 6.1 %fusion.6 = bf16[1,192,4096]{2,1,0:T(8,128)(2,1)} fusion(f32[2,192,4096]{2,1,0:T(8,128)} %copy-done.1, s32[]{:T(128)S(6)} %select_n.25, bf16[2,192,4096]{2,1,0:T(8,128)(2,1)} %all-gather.5.cloned.1.call-done, bf16[2,192,4096]{2,1,0:T(8,128)(2,1)} %all-gather.3.cloned.1.call-done), kind=kLoop, calls=%fused_computation.14 | loop fusion | flops 10223616 | bytes 7864324 | tf_op jit(solution)/shard_map/convert_element_type | solution.py:141
  (47 shorter events, 4.4 us)
Async XLA Ops:
  7.2 74.0 %copy-start = (bf16[1,4096,192]{1,2,0:T(8,128)(2,1)S(1)}, bf16[1,4096,192]{1,2,0:T(8,128)(2,1)}, u32[]{:S(2)}) copy-start(bf16[1,4096,192]{1,2,0:T(8,128)(2,1)} %param.14) | copy-start | bytes 4718596
  11.9 10.5 %all-to-all-start = ((bf16[16,1,24]{2,1,0:T(2,128)(2,1)}), bf16[16,1,24]{2,1,0:T(2,128)(2,1)S(1)}, u32[]{:S(2)}, u32[]{:S(2)}) async-start(bf16[16,1,24]{2,1,0:T(2,128)(2,1)} %copy.29), calls=%async_computation | async-start | bytes 16384 | tf_op jit(solution)/shard_map/all_to_all | solution.py:75
  24.5 48.6 %all-to-all-start.2 = ((bf16[16,24,4096]{2,1,0:T(8,128)(2,1)}), bf16[16,24,4096]{2,1,0:T(8,128)(2,1)}, u32[]{:S(2)}, u32[]{:S(2)}) async-start(bf16[16,24,4096]{2,1,0:T(8,128)(2,1)} %bitcast.62), calls=%async_computation.2 | async-start | bytes 6291456 | tf_op jit(solution)/shard_map/all_to_all | solution.py:73
  75.1 4.6 copy-start.8
  75.2 47.2 %all-to-all-start.1 = ((bf16[16,24,4096]{2,1,0:T(8,128)(2,1)}), bf16[16,24,4096]{2,1,0:T(8,128)(2,1)}, u32[]{:S(2)}, u32[]{:S(2)}) async-start(bf16[16,24,4096]{2,1,0:T(8,128)(2,1)} %bitcast.60), calls=%async_computation.1 | async-start | bytes 6291456 | tf_op jit(solution)/shard_map/all_to_all | solution.py:74
  79.7 4.5 copy-start.2
  79.7 230.2 %all-reduce.3.cloned.1.call-start = ((), (), s32[]{:S(2)}) async-start(), calls=%async_computation.5 | async-start | bytes 6291456 | tf_op jit(solution)/shard_map/psum | solution.py:123
  122.3 2.9 copy-start.3
  128.5 292.1 %all-gather.3.cloned.1.call-start = ((), (), s32[]{:S(2)}) async-start(), calls=%async_computation.4 | async-start | bytes 3342336 | tf_op jit(solution)/shard_map/all_gather | solution.py:125
  309.9 5.4 %copy-start.5 = (f32[2,192,256]{2,1,0:T(8,128)S(1)}, f32[2,192,256]{2,1,0:T(8,128)}, u32[]{:S(2)}) copy-start(f32[2,192,256]{2,1,0:T(8,128)} %param.19) | copy-start | bytes 1179652
  309.9 5.4 %copy-start.6 = (f32[2,192,256]{2,1,0:T(8,128)S(1)}, f32[2,192,256]{2,1,0:T(8,128)}, u32[]{:S(2)}) copy-start(f32[2,192,256]{2,1,0:T(8,128)} %param.18) | copy-start | bytes 1179652
  312.7 2.7 copy-start.1
  316.4 198.4 %all-gather.5.cloned.1.call-start = ((), (), s32[]{:S(2)}) async-start(), calls=%async_computation.6 | async-start | bytes 3342336 | tf_op jit(solution)/shard_map/all_gather | solution.py:128
  317.2 3.0 copy-start.7
  320.2 1.2 copy-start.4
  325.3 47.5 %all-to-all-start.3 = ((bf16[16,24,4096]{2,1,0:T(8,128)(2,1)}), bf16[16,24,4096]{2,1,0:T(8,128)(2,1)}, u32[]{:S(2)}, u32[]{:S(2)}) async-start(bf16[16,24,4096]{2,1,0:T(8,128)(2,1)} %bitcast.61), calls=%async_computation.3 | async-start | bytes 6291456 | tf_op jit(solution)/shard_map/all_to_all | solution.py:106
Sparse Core Ops, SparseCore 0:
  128.7 181.2 all-reduce.2
  316.6 104.0 all-gather.2
  423.1 91.6 all-gather.4
where the time goes:
time: 528 us; the launch traced here: 527 us
  waiting for transfers between devices  439 us (83%)
  other arithmetic  22.7 us (4%)
  starting transfers between devices  20.7 us (4%)
  matrix products  20.5 us (4%)
  between operations  16 us (3%)
  local copies, waits for them, and re-layouts  8.52 us (2%)
    psum x1, waiting for transfers between devices, body(): lax.psum(cand_grads.astype(jnp.bfloat16), 'grp').astype(jnp.float32)  181 us
    all_gather x1, waiting for transfers between devices, body(): lax.all_gather(moment_second.astype(jnp.bfloat16), 'grp', axis=2, tiled=T...  94.2 us
    all_gather x1, waiting for transfers between devices, body(): lax.all_gather(moment_first.astype(jnp.bfloat16), 'grp', axis=2, tiled=True)  43.8 us
    all_to_all x1, waiting for transfers between devices, body(): lax.all_to_all(spread(send_tokens), 'ep', split_axis=0, concat_axis=0, ti...  41.2 us
    all_to_all x1, waiting for transfers between devices, body(): lax.all_to_all(partial_value.reshape(num_ep, CAP, width), 'ep', split_axi...  40.9 us
    all_to_all x1, waiting for transfers between devices, body(): lax.all_to_all(spread(send_grads), 'ep', split_axis=0, concat_axis=0, til...  34.3 us
  transfers between devices with their start and end apart: 7, of which 7 were waited for; matrix products, arithmetic and copies ran while one was open for 5% of the time, Pallas kernels for 0%

commit v1 on v0

--- a/solution.py
+++ b/solution.py
@@ -12,6 +12,11 @@
 adam_eps = 1e-08
 first_fix = 1.0 - math.exp(1000.0 * math.log(0.9))
 second_fix = 1.0 - math.exp(1000.0 * math.log(0.999))
+
+
+def summed_here(x, name):
+    terms = lax.all_gather(x, name)
+    return jnp.sum(terms, axis=0)
 
 
 def moments(gradient, first_moment, second):
@@ -120,7 +125,7 @@
     my_cand = lax.dynamic_index_in_dim(placement[0], ep_index // QUARTERS, 0, keepdims=False)
     cand_mask = (jnp.arange(CANDS, dtype=jnp.int32) == my_cand).astype(jnp.float32)
     cand_grads = cand_mask[:, None, None] * weight_grad[None]
-    totals = lax.psum(cand_grads.astype(jnp.bfloat16), "grp").astype(jnp.float32)
+    totals = summed_here(cand_grads.astype(jnp.bfloat16), "grp").astype(jnp.float32)
     full_first, full_second = (
         lax.all_gather(moment_first.astype(jnp.bfloat16), "grp", axis=2, tiled=True).astype(
             moment_first.dtype

time: 528 us -> 968 us (1.83)
  waiting for transfers between devices: 439 us -> 860 us
  other arithmetic: 22.7 us -> 40.9 us
    all_gather x0 -> x1, waiting for transfers between devices: none -> 602 us  [summed_here(): terms = lax.all_gather(x, name)]
    psum x1 -> x0, waiting for transfers between devices: 181 us -> none  [body(): lax.psum(cand_grads.astype(jnp.bfloat16), 'grp').astype(jnp.float32)]
    reduce_sum x0 -> x1, other arithmetic: none -> 18.3 us  [summed_here(): return jnp.sum(terms, axis=0)]
  transfers between devices with their start and end apart: 7 -> 7, of which waited for: 7 -> 7; matrix products, arithmetic and copies ran while one was open for 5% -> 2% of each run, Pallas kernels for 0% -> 0%
where the time goes in v1:
time: 968 us; the launch traced here: 967 us
  waiting for transfers between devices  860 us (89%)
  other arithmetic  40.9 us (4%)
  starting transfers between devices  21.2 us (2%)
  matrix products  20.5 us (2%)
  between operations  15.9 us (2%)
    all_gather x1, waiting for transfers between devices, summed_here(): terms = lax.all_gather(x, name)  602 us
    all_gather x1, waiting for transfers between devices, body(): lax.all_gather(moment_second.astype(jnp.bfloat16), 'grp', axis=2, tiled=T...  94.2 us
    all_gather x1, waiting for transfers between devices, body(): lax.all_gather(moment_first.astype(jnp.bfloat16), 'grp', axis=2, tiled=True)  43.7 us
    all_to_all x1, waiting for transfers between devices, body(): lax.all_to_all(spread(send_tokens), 'ep', split_axis=0, concat_axis=0, ti...  41.2 us
    all_to_all x1, waiting for transfers between devices, body(): lax.all_to_all(partial_value.reshape(num_ep, CAP, width), 'ep', split_axi...  41 us
    all_to_all x1, waiting for transfers between devices, body(): lax.all_to_all(spread(send_grads), 'ep', split_axis=0, concat_axis=0, til...  34.3 us
  transfers between devices with their start and end apart: 7, of which 7 were waited for; matrix products, arithmetic and copies ran while one was open for 2% of the time, Pallas kernels for 0%

profile of v1, /device:TPU:2, one launch (start us, length us, event | category | flops | bytes accessed | tf_op | source)
XLA Modules:
  0.0 966.9 jit_solution(667143558733277540)
XLA Ops:
  8.7 0.8 fusion.24
  9.6 1.2 reduce-window.6
  11.9 5.9 all-to-all-start
  18.0 1.8 convolution_convert_fusion.1
  19.8 2.6 all-to-all-done
  22.4 2.1 broadcast_in_dim.53
  24.5 5.7 all-to-all-start.2
  30.2 1.8 convolution_convert_fusion.2
  31.9 41.2 %all-to-all-done.2 = bf16[16,24,4096]{2,1,0:T(8,128)(2,1)} async-done(((bf16[16,24,4096]{2,1,0:T(8,128)(2,1)}), bf16[16,24,4096]{2,1,0:T(8,128)(2,1)}, u32[]{:S(2)}, u32[]{:S(2)}) %all-to-all-start.2) | async-done | bytes 3145760 | tf_op jit(solution)/shard_map/all_to_all | solution.py:78
  73.1 2.1 broadcast_in_dim.29
  75.2 4.5 all-to-all-start.1
  81.2 3.1 fusion.9
  84.2 3.8 fusion.12
  88.0 34.3 %all-to-all-done.1 = bf16[16,24,4096]{2,1,0:T(8,128)(2,1)} async-done(((bf16[16,24,4096]{2,1,0:T(8,128)(2,1)}), bf16[16,24,4096]{2,1,0:T(8,128)(2,1)}, u32[]{:S(2)}, u32[]{:S(2)}) %all-to-all-start.1) | async-done | bytes 3145760 | tf_op jit(solution)/shard_map/all_to_all | solution.py:79
  122.3 2.9 fusion
  125.3 1.0 fusion.18
  126.3 2.2 multiply_convert_fusion
  128.5 602.3 %all-gather.6.cloned.1.call-done = bf16[16,2,192,4096]{3,2,1,0:T(8,128)(2,1)} async-done(((bf16[1,2,192,4096]{3,2,1,0:T(8,128)(2,1)}), bf16[16,2,192,4096]{3,2,1,0:T(8,128)(2,1)}) %all-gather.6.cloned.1.call-update) | async-done | bytes 50331664 | tf_op jit(solution)/shard_map/all_gather | solution.py:18
  730.9 18.3 %reduce_sum.32 = bf16[2,192,4096]{2,1,0:T(8,128)(2,1)} reduce(bf16[16,2,192,4096]{3,2,1,0:T(8,128)(2,1)} %all-gather.6.cloned.1.call-done, bf16[]{:T(256)} %constant.67.clone.1), dimensions={0}, to_apply=%region_5.6 | reduce | flops 23592960 | bytes 53477376 | tf_op jit(solution)/shard_map/reduce_sum | solution.py:19
  749.2 2.7 convert_element_type.133
  751.9 2.7 copy-done.1
  754.6 1.1 fusion.16
  756.4 3.0 multiply_convert_fusion.1
  759.5 1.2 fusion.14
  760.7 1.1 fusion.7
  761.8 2.7 add_convert_fusion
  764.5 4.8 all-to-all-start.3
  771.3 41.0 %all-to-all-done.3 = bf16[16,24,4096]{2,1,0:T(8,128)(2,1)} async-done(((bf16[16,24,4096]{2,1,0:T(8,128)(2,1)}), bf16[16,24,4096]{2,1,0:T(8,128)(2,1)}, u32[]{:S(2)}, u32[]{:S(2)}) %all-to-all-start.3) | async-done | bytes 3145760 | tf_op jit(solution)/shard_map/all_to_all | solution.py:111
  812.4 4.1 convolution_convert_fusion
  816.4 43.7 %all-gather.4.cloned.1.call-done = bf16[2,192,4096]{2,1,0:T(8,128)(2,1)} async-done(((bf16[2,192,256]{2,1,0:T(8,128)(2,1)}), bf16[2,192,4096]{2,1,0:T(8,128)(2,1)}) %all-gather.4.cloned.1.call-update) | async-done | bytes 3145744 | tf_op jit(solution)/shard_map/all_gather | solution.py:130
  860.2 94.2 %all-gather.8.cloned.1.call-done = bf16[2,192,4096]{2,1,0:T(8,128)(2,1)} async-done(((bf16[2,192,256]{2,1,0:T(8,128)(2,1)}), bf16[2,192,4096]{2,1,0:T(8,128)(2,1)}) %all-gather.8.cloned.1.call-update) | async-done | bytes 3145744 | tf_op jit(solution)/shard_map/all_gather | solution.py:133
  954.3 6.1 fusion.6
  (48 shorter events, 5.2 us)
Async XLA Ops:
  7.2 74.0 %copy-start = (bf16[1,4096,192]{1,2,0:T(8,128)(2,1)S(1)}, bf16[1,4096,192]{1,2,0:T(8,128)(2,1)}, u32[]{:S(2)}) copy-start(bf16[1,4096,192]{1,2,0:T(8,128)(2,1)} %param.14) | copy-start | bytes 4718596
  11.9 10.5 %all-to-all-start = ((bf16[16,1,24]{2,1,0:T(2,128)(2,1)}), bf16[16,1,24]{2,1,0:T(2,128)(2,1)S(1)}, u32[]{:S(2)}, u32[]{:S(2)}) async-start(bf16[16,1,24]{2,1,0:T(2,128)(2,1)} %copy.29), calls=%async_computation | async-start | bytes 16384 | tf_op jit(solution)/shard_map/all_to_all | solution.py:80
  24.5 48.6 %all-to-all-start.2 = ((bf16[16,24,4096]{2,1,0:T(8,128)(2,1)}), bf16[16,24,4096]{2,1,0:T(8,128)(2,1)}, u32[]{:S(2)}, u32[]{:S(2)}) async-start(bf16[16,24,4096]{2,1,0:T(8,128)(2,1)} %bitcast.62), calls=%async_computation.2 | async-start | bytes 6291456 | tf_op jit(solution)/shard_map/all_to_all | solution.py:78
  75.1 4.6 copy-start.8
  75.2 47.2 %all-to-all-start.1 = ((bf16[16,24,4096]{2,1,0:T(8,128)(2,1)}), bf16[16,24,4096]{2,1,0:T(8,128)(2,1)}, u32[]{:S(2)}, u32[]{:S(2)}) async-start(bf16[16,24,4096]{2,1,0:T(8,128)(2,1)} %bitcast.60), calls=%async_computation.1 | async-start | bytes 6291456 | tf_op jit(solution)/shard_map/all_to_all | solution.py:79
  79.7 4.5 copy-start.2
  79.7 651.2 %all-gather.6.cloned.1.call-start = ((), (), s32[]{:S(2)}) async-start(), calls=%async_computation.5 | async-start | bytes 53477376 | tf_op jit(solution)/shard_map/all_gather | solution.py:18
  122.3 2.9 copy-start.3
  128.5 731.7 %all-gather.4.cloned.1.call-start = ((), (), s32[]{:S(2)}) async-start(), calls=%async_computation.4 | async-start | bytes 3342336 | tf_op jit(solution)/shard_map/all_gather | solution.py:130
  749.2 5.4 copy-start.5
  749.2 5.4 copy-start.6
  751.9 2.7 copy-start.1
  755.7 198.7 %all-gather.8.cloned.1.call-start = ((), (), s32[]{:S(2)}) async-start(), calls=%async_computation.6 | async-start | bytes 3342336 | tf_op jit(solution)/shard_map/all_gather | solution.py:133
  756.4 3.0 copy-start.7
  759.5 1.2 copy-start.4
  764.5 47.8 %all-to-all-start.3 = ((bf16[16,24,4096]{2,1,0:T(8,128)(2,1)}), bf16[16,24,4096]{2,1,0:T(8,128)(2,1)}, u32[]{:S(2)}, u32[]{:S(2)}) async-start(bf16[16,24,4096]{2,1,0:T(8,128)(2,1)} %bitcast.61), calls=%async_computation.3 | async-start | bytes 6291456 | tf_op jit(solution)/shard_map/all_to_all | solution.py:111
Sparse Core Ops, SparseCore 0:
  128.6 602.2 all-gather.5
  755.8 104.3 all-gather.3
  862.6 91.6 all-gather.7
